TPU v7x, 32 devices: a whole 2x2x4 slice. The times are simulated.
32 devices in a mesh: groups: 2 (over x), row: 16 (over z, y, core).
Axes of the slice: x: 2, y: 2, z: 4, core: 2. Of those that a mesh axis runs over, the one named last changes fastest.
Arguments:
- inverse: float32 [4, 4096, 4096], P('groups', 'row'), parts along dimension 0, as said below
- cycle: bfloat16 [4, 4096, 1024], P('groups', 'row'), parts along dimension 0, as said below
- arrivals: bfloat16 [4, 2, 4096, 128], P('groups', None, 'row'), parts along dimension 0, may hold values from -6 to 6
- departing: int32 [4, 128], P('groups'), parts along dimension 0, may hold values from 0 to 1023, as said below
- directions: int32 [4, 512], P('groups'), parts along dimension 0, may hold values from 0 to 8191
Outputs:
- new_inverse: float32 [4, 4096, 4096], P('groups', 'row'), parts along dimension 0
- beam_weights: float32 [4, 2, 4096, 512], P('groups', None, 'row'), parts along dimension 0
- spectrum: float32 [4, 512], P('groups'), parts along dimension 0
There are 2 independent parts, one for each index of `groups`. A program takes and returns all parts, laid end to end along the dimension named above; each array names one. Nothing has to cross between parts.
Inputs may be any that keep to these rules, and one draw needn't show every extreme that they name: inverse is Hermitian and is the inverse of I + cycle cycle^H / 1024. `cycle`: the snapshots whose inverse covariance is given. `departing`: all 2 x 128 entries are different slots.
All inputs are finite; a program needn't handle non-finite values.
Results may differ from a plain program's by a relative error of at most 0.0003.
Values may be sent and summed in bfloat16 or wider, within the bound.
A program may use at most 192 MiB of HBM per device.

v0:
```python
import jax
import jax.numpy as jnp
from jax import lax
from jax.sharding import PartitionSpec as P

M = 4096
CYCLE = 1024
STEPS = 2


precise = lax.Precision.HIGHEST


def matmul(left, right):
    return jnp.dot(left, right, precision=precise, preferred_element_type=jnp.float32)


def lead_dot(left, right):
    return lax.dot_general(
        left, right, (((0,), (0,)), ((), ())), precision=precise, preferred_element_type=jnp.float32
    )


def tail_dot(left, right):
    return lax.dot_general(
        left, right, (((1,), (1,)), ((), ())), precision=precise, preferred_element_type=jnp.float32
    )


def complex_mul(left_re, left_im, right_re, right_im):
    return (
        matmul(left_re, right_re) - matmul(left_im, right_im),
        matmul(left_re, right_im) + matmul(left_im, right_re),
    )


def steering(direction_ids, length):
    element = jnp.arange(length, dtype=jnp.int32)[:, None]
    odd_index = 2 * direction_ids[None, :] + 1
    angle_count = 2 * length
    turns = (element * odd_index - element * angle_count) % (2 * angle_count)
    phase = jnp.pi * turns.astype(jnp.float32) / angle_count
    return (jnp.cos(phase), jnp.sin(phase))


def hermitian_solve(herm_re, herm_im, rhs_re, rhs_im):
    order = herm_re.shape[0]
    embedded = jnp.concatenate(
        [jnp.concatenate([herm_re, -herm_im], 1), jnp.concatenate([herm_im, herm_re], 1)], 0
    )
    factor = jnp.linalg.cholesky(embedded)
    solution = jax.scipy.linalg.cho_solve((factor, True), jnp.concatenate([rhs_re, rhs_im], 0))
    return (solution[:order], solution[order:])


def block_product(current, snap_block):
    inv_re, inv_im = current
    piece_wide = lax.all_gather(snap_block, "row", axis=1, tiled=True).astype(jnp.float32)
    new_re = matmul(inv_re, piece_wide[0]) - matmul(inv_im, piece_wide[1])
    new_im = matmul(inv_re, piece_wide[1]) + matmul(inv_im, piece_wide[0])
    return (new_re, new_im)


def capacitance(snap_block, q_re, q_im):
    snap_wide = snap_block.astype(jnp.float32)
    cap_re = lead_dot(snap_wide[0], q_re) + lead_dot(snap_wide[1], q_im)
    cap_im = lead_dot(snap_wide[0], q_im) - lead_dot(snap_wide[1], q_re)
    return lax.psum((cap_re, cap_im), "row")


def apply_update(current, q_re, q_im, fold_re, fold_im):
    inv_re, inv_im = current
    shard_piece = lax.all_gather(jnp.stack([q_re, q_im]), "row", axis=1, tiled=True)
    new_re = inv_re - tail_dot(fold_re, shard_piece[0]) - tail_dot(fold_im, shard_piece[1])
    new_im = inv_im - tail_dot(fold_im, shard_piece[0]) + tail_dot(fold_re, shard_piece[1])
    updated = jnp.stack([new_re, new_im])
    return (updated[0], updated[1])


def joint_update(current, snap_block):
    q_re, q_im = block_product(current, snap_block)
    cap_re, cap_im = capacitance(snap_block, q_re, q_im)
    half = snap_block.shape[2] // 2
    identity = CYCLE * jnp.eye(half, dtype=jnp.float32)
    rhs_re, rhs_im = (q_re.T, -q_im.T)
    col_count = rhs_re.shape[1]
    first_re, first_im = hermitian_solve(
        identity + cap_re[:half, :half],
        cap_im[:half, :half],
        jnp.concatenate([rhs_re[:half], cap_re[:half, half:]], 1),
        jnp.concatenate([rhs_im[:half], cap_im[:half, half:]], 1),
    )
    base_re, base_im = (first_re[:, :col_count], first_im[:, :col_count])
    cross_re, cross_im = (first_re[:, col_count:], first_im[:, col_count:])
    prod_re, prod_im = complex_mul(cap_re[half:, :half], cap_im[half:, :half], cross_re, cross_im)
    schur_re = identity - cap_re[half:, half:] + prod_re
    schur_im = -cap_im[half:, half:] + prod_im
    lower_re, lower_im = complex_mul(cap_re[half:, :half], cap_im[half:, :half], base_re, base_im)
    second_re, second_im = hermitian_solve(
        schur_re, schur_im, rhs_re[half:] - lower_re, rhs_im[half:] - lower_im
    )
    upper_re, upper_im = complex_mul(cross_re, cross_im, -second_re, -second_im)
    sol_re = jnp.concatenate([base_re - upper_re, -second_re], 0)
    sol_im = jnp.concatenate([base_im - upper_im, -second_im], 0)
    return apply_update(current, q_re, q_im, sol_re.T, -sol_im.T)


def on_device(inverse, cycle, arrivals, departing, directions):
    current = (inverse[0], inverse[1])
    row_count = inverse.shape[1]
    first_row = lax.axis_index("row") * row_count
    weight_list = []
    power_list = []
    for step_index in range(STEPS):
        steer_re, steer_im = steering(directions[step_index], M)
        local_re = lax.dynamic_slice_in_dim(steer_re, first_row, row_count, 0)
        local_im = lax.dynamic_slice_in_dim(steer_im, first_row, row_count, 0)
        app_re, app_im = complex_mul(current[0], current[1], steer_re, steer_im)
        partial_power = jnp.sum(local_re * app_re + local_im * app_im, axis=0)
        power = lax.psum(partial_power, "row")
        departed = jnp.take(cycle, departing[step_index], axis=2)
        current = joint_update(current, jnp.concatenate([arrivals[step_index], departed], axis=2))
        weight_list.append(jnp.stack([M * app_re / power, M * app_im / power]))
        power_list.append(M / power)
    return (jnp.stack([current[0], current[1]]), jnp.stack(weight_list), jnp.stack(power_list))


def solution(mesh):
    in_specs = (
        P("groups", "row", None),
        P("groups", "row", None),
        P("groups", None, "row", None),
        P("groups", None),
        P("groups", None),
    )
    out_specs = (P("groups", "row", None), P("groups", None, "row", None), P("groups", None))
    return jax.shard_map(
        on_device, mesh=mesh, in_specs=in_specs, out_specs=out_specs, check_vma=False
    )
```

profile of v0, /device:TPU:0, one launch (start us, length us, event | category | flops | bytes accessed | tf_op | source)
XLA Modules:
  0.0 945.6 jit_solution(2639609312674014120)
XLA Ops:
  26.9 44.0 %fusion.14 = f32[512,256]{0,1:T(8,128)S(1)} fusion(s32[4096]{0:T(1024)S(1)} %iota_multiply_fusion, s32[512]{0:T(512)S(1)} %bitcast.363, f32[256,4096]{1,0:T(8,128)} %fusion.361), kind=kOutput, calls=%fused_computation.43 | convolution fusion | flops 6473908224 | bytes 4737024 | tf_op jit(solution)/shard_map/dot_general | solution.py:15
  71.0 52.9 %fusion.12 = f32[512,256]{0,1:T(8,128)} fusion(s32[4096]{0:T(1024)S(1)} %iota_multiply_fusion, s32[512]{0:T(512)S(1)} %bitcast.364, f32[256,4096]{1,0:T(8,128)S(1)} %copy-done.11), kind=kOutput, calls=%fused_computation.41 | convolution fusion | flops 6473908224 | bytes 4737024 | tf_op jit(solution)/shard_map/dot_general | solution.py:15
  123.8 52.9 %fusion.71 = f32[256,512]{1,0:T(8,128)} fusion(f32[512,256]{0,1:T(8,128)S(1)} %fusion.14, s32[4096]{0:T(1024)S(1)} %iota_multiply_fusion, s32[512]{0:T(512)S(1)} %bitcast.365, f32[256,4096]{1,0:T(8,128)S(1)} %copy-done.10), kind=kOutput, calls=%fused_computation.85 | convolution fusion | flops 6474039296 | bytes 5261312 | tf_op jit(solution)/shard_map/dot_general | solution.py:15
  176.7 14.3 %fusion.275 = (bf16[1,4096,256]{1,0,2:T(2,128)(2,1)}, bf16[1,4096,256]{1,0,2:T(2,128)(2,1)}) fusion(bf16[2,4096,256]{1,0,2:T(2,128)(2,1)} %all-gather.5.cloned.1.call-done), kind=kLoop, calls=%fused_computation.391 | loop fusion | bytes 8388608 | tf_op jit(solution)/shard_map/slice | solution.py:59
  237.1 68.7 %fusion.11 = (f32[4096,512]{1,0:T(8,128)S(1)}, f32[4096,512]{1,0:T(8,128)S(1)}, f32[4096,512]{1,0:T(8,128)}, f32[4096,512]{1,0:T(8,128)}) fusion(s32[4096]{0:T(1024)S(1)} %iota_multiply_fusion, s32[512]{0:T(512)S(1)} %bitcast.366, s32[512]{0:T(512)S(1)} %bitcast.358), kind=kLoop, calls=%fused_computation.36 | loop fusion | flops 62914560 | bytes 33574912 | tf_op jit(solution)/shard_map/cos | solution.py:43
  305.8 40.4 %add_reduce_fusion.1 = (f32[512]{0:T(512)}, f32[256,512]{1,0:T(8,128)}) fusion(f32[4096,512]{1,0:T(8,128)S(1)} %get-tuple-element.126, s32[]{:T(128)S(6)} %select_n.28, f32[256,512]{1,0:T(8,128)S(1)} %copy-done.19, f32[4096,512]{1,0:T(8,128)S(1)} %get-tuple-element.125, f32[512,256]{0,1:T(8,128)S(1)} %copy-done.28, s32[4096]{0:T(1024)S(1)} %iota_multiply_fusion, ...), kind=kOutput, calls=%fused_computation.143 | convolution fusion | flops 6474563072 | bytes 6836228 | tf_op jit(solution)/shard_map/dot_general | solution.py:15
  379.4 11.7 %cholesky.214 = f32[128,128]{1,0:T(8,128)S(1)} custom-call(f32[128,128]{1,0:T(8,128)S(1)} %cholesky.346), custom_call_target="Cholesky" | custom-call | tf_op jit(solution)/shard_map/jit(cholesky)/cholesky | solution.py:51
  401.5 11.7 %cholesky.231 = f32[128,128]{1,0:T(8,128)S(1)} custom-call(f32[128,128]{1,0:T(8,128)S(1)} %convolution_subtract_fusion.25), custom_call_target="Cholesky" | custom-call | tf_op jit(solution)/shard_map/jit(cholesky)/cholesky | solution.py:51
  420.5 20.1 %custom-call.24 = f32[2,128,128]{1,2,0:T(8,128)S(1)} custom-call(f32[2,128,128]{2,1,0:T(8,128)S(1)} %get-tuple-element.35), custom_call_target="InvertDiagBlocksLowerTriangular" | custom-call | tf_op jit(solution)/shard_map/jit(_cho_solve)/triangular_solve | solution.py:52
  452.7 11.7 %cholesky.248 = f32[128,128]{1,0:T(8,128)S(1)} custom-call(f32[128,128]{1,0:T(8,128)S(1)} %cholesky.349), custom_call_target="Cholesky" | custom-call | tf_op jit(solution)/shard_map/jit(cholesky)/cholesky | solution.py:51
  476.4 11.9 %cholesky.265 = f32[128,128]{1,0:T(8,128)S(1)} custom-call(f32[128,128]{1,0:T(8,128)S(1)} %convolution_subtract_fusion.23), custom_call_target="Cholesky" | custom-call | tf_op jit(solution)/shard_map/jit(cholesky)/cholesky | solution.py:51
  496.8 19.7 %custom-call.26 = f32[2,128,128]{1,2,0:T(8,128)S(1)} custom-call(f32[2,128,128]{2,1,0:T(8,128)S(1)} %get-tuple-element.36), custom_call_target="InvertDiagBlocksLowerTriangular" | custom-call | tf_op jit(solution)/shard_map/jit(_cho_solve)/triangular_solve | solution.py:52
  535.7 39.2 %fusion.30 = f32[256,512]{1,0:T(8,128)} fusion(f32[256,4096]{1,0:T(8,128)S(1)} %convolution_subtract_fusion.4, s32[512]{0:T(512)S(1)} %bitcast.359, s32[4096]{0:T(1024)S(1)} %iota_multiply_fusion), kind=kOutput, calls=%fused_computation.58 | convolution fusion | flops 6473908224 | bytes 4737024 | tf_op jit(solution)/shard_map/dot_general | solution.py:15
  595.3 43.5 %fusion.28 = f32[256,512]{1,0:T(8,128)S(1)} fusion(f32[256,4096]{1,0:T(8,128)} %copy-done.3, s32[512]{0:T(512)S(1)} %bitcast.360, s32[4096]{0:T(1024)S(1)} %iota_multiply_fusion), kind=kOutput, calls=%fused_computation.57 | convolution fusion | flops 6473908224 | bytes 4737024 | tf_op jit(solution)/shard_map/dot_general | solution.py:15
  638.8 38.5 %fusion.60 = f32[256,512]{1,0:T(8,128)S(1)} fusion(f32[256,512]{1,0:T(8,128)S(1)} %copy-done.29, f32[256,4096]{1,0:T(8,128)S(1)} %copy-done.4, s32[512]{0:T(512)S(1)} %bitcast.361, s32[4096]{0:T(1024)S(1)} %iota_multiply_fusion), kind=kOutput, calls=%fused_computation.82 | convolution fusion | flops 6474039296 | bytes 5261312 | tf_op jit(solution)/shard_map/dot_general | solution.py:15
  677.3 53.5 %add_reduce_fusion = (f32[512]{0:T(512)S(1)}, f32[256,512]{1,0:T(8,128)S(1)}) fusion(f32[4096,512]{1,0:T(8,128)} %get-tuple-element.129, s32[]{:T(128)S(6)} %select_n.28, f32[256,512]{1,0:T(8,128)S(1)} %fusion.60, f32[4096,512]{1,0:T(8,128)} %get-tuple-element.130, f32[256,512]{1,0:T(8,128)S(1)} %fusion.28, f32[256,4096]{1,0:T(8,128)S(1)} %copy-done.2, ...), kind=kOutput, calls=%fused_computation.140 | convolution fusion | flops 6474563072 | bytes 6836228 | tf_op jit(solution)/shard_map/dot_general | solution.py:15
  730.8 35.8 %all-reduce.1 = (f32[512]{0:T(512)S(1)}, f32[512]{0:T(512)S(1)}) all-reduce(f32[512]{0:T(512)S(1)} %get-tuple-element.157, f32[512]{0:T(512)S(1)} %copy-done.25), channel_id=1, replica_groups=mesh['groups'=2,'row'=16] {'row'}, use_global_device_ids=true, to_apply=%region_11.16 | all-reduce | flops 1024 | bytes 8192 | tf_op jit(solution)/shard_map/psum | solution.py:120
  771.3 11.7 %cholesky.282 = f32[128,128]{1,0:T(8,128)S(1)} custom-call(f32[128,128]{1,0:T(8,128)S(1)} %cholesky.352), custom_call_target="Cholesky" | custom-call | tf_op jit(solution)/shard_map/jit(cholesky)/cholesky | solution.py:51
  793.3 11.7 %cholesky.299 = f32[128,128]{1,0:T(8,128)S(1)} custom-call(f32[128,128]{1,0:T(8,128)S(1)} %convolution_subtract_fusion.22), custom_call_target="Cholesky" | custom-call | tf_op jit(solution)/shard_map/jit(cholesky)/cholesky | solution.py:51
  812.0 19.8 %custom-call.28 = f32[2,128,128]{1,2,0:T(8,128)S(1)} custom-call(f32[2,128,128]{2,1,0:T(8,128)S(1)} %get-tuple-element.37), custom_call_target="InvertDiagBlocksLowerTriangular" | custom-call | tf_op jit(solution)/shard_map/jit(_cho_solve)/triangular_solve | solution.py:52
  836.4 11.7 %cholesky.316 = f32[128,128]{1,0:T(8,128)S(1)} custom-call(f32[128,128]{1,0:T(8,128)S(1)} %cholesky.355), custom_call_target="Cholesky" | custom-call | tf_op jit(solution)/shard_map/jit(cholesky)/cholesky | solution.py:51
  858.5 11.9 %cholesky.333 = f32[128,128]{1,0:T(8,128)S(1)} custom-call(f32[128,128]{1,0:T(8,128)S(1)} %convolution_subtract_fusion.20), custom_call_target="Cholesky" | custom-call | tf_op jit(solution)/shard_map/jit(cholesky)/cholesky | solution.py:51
  877.3 19.7 %custom-call.30 = f32[2,128,128]{1,2,0:T(8,128)S(1)} custom-call(f32[2,128,128]{2,1,0:T(8,128)S(1)} %get-tuple-element.38), custom_call_target="InvertDiagBlocksLowerTriangular" | custom-call | tf_op jit(solution)/shard_map/jit(_cho_solve)/triangular_solve | solution.py:52
  901.6 12.5 %convolution_subtract_fusion.2 = f32[256,4096]{1,0:T(8,128)S(1)} fusion(f32[256,4096]{1,0:T(8,128)} %copy-done.1, f32[2,4096,256]{2,1,0:T(8,128)} %all-gather.11.cloned.1.call-done, f32[128,256]{1,0:T(8,128)S(1)} %convolution_negate_fusion, f32[128,256]{1,0:T(8,128)S(1)} %fusion.108), kind=kOutput, calls=%fused_computation.28 | convolution fusion | flops 3222339584 | bytes 12845056 | tf_op jit(solution)/shard_map/dot_general | solution.py:25
  (297 shorter events, 272.1 us)
Async XLA Ops:
  7.2 169.6 %all-gather.5.cloned.1.call-start = ((), (), s32[]{:S(2)}) async-start(), calls=%async_computation | async-start | bytes 4456448 | tf_op jit(solution)/shard_map/all_gather | solution.py:58
  13.8 333.1 %all-gather.9.cloned.1.call-start = ((), (), s32[]{:S(2)}) async-start(), calls=%async_computation.2 | async-start | bytes 4456448 | tf_op jit(solution)/shard_map/all_gather | solution.py:58
  16.2 361.4 %all-reduce.9.cloned.1.call-start = ((), (), s32[]{:S(2)}) async-start(), calls=%async_computation.5 | async-start | bytes 1048576 | tf_op jit(solution)/shard_map/psum | solution.py:68
  26.9 210.2 %copy-start.22 = (s32[1,512]{1,0:T(1,128)}, s32[1,512]{1,0:T(1,128)S(1)}, u32[]{:S(2)}) copy-start(s32[1,512]{1,0:T(1,128)S(1)} %get-tuple-element.132) | copy-start | bytes 6148
  26.9 44.0 %copy-start.11 = (f32[256,4096]{1,0:T(8,128)S(1)}, f32[256,4096]{1,0:T(8,128)}, u32[]{:S(2)}) copy-start(f32[256,4096]{1,0:T(8,128)} %fusion.359) | copy-start | bytes 12582916
  70.9 52.9 %copy-start.10 = (f32[256,4096]{1,0:T(8,128)S(1)}, f32[256,4096]{1,0:T(8,128)}, u32[]{:S(2)}) copy-start(f32[256,4096]{1,0:T(8,128)} %fusion.363) | copy-start | bytes 12582916
  232.1 292.0 %all-gather.7.cloned.1.call-start = ((), (), s32[]{:S(2)}) async-start(), calls=%async_computation.1 | async-start | bytes 8912896 | tf_op jit(solution)/shard_map/all_gather | solution.py:73
  234.5 534.7 %all-reduce.7.cloned.1.call-start = ((), (), s32[]{:S(2)}) async-start(), calls=%async_computation.4 | async-start | bytes 1048576 | tf_op jit(solution)/shard_map/psum | solution.py:68
  237.1 68.7 %copy-start.19 = (f32[256,512]{1,0:T(8,128)S(1)}, f32[256,512]{1,0:T(8,128)}, u32[]{:S(2)}) copy-start(f32[256,512]{1,0:T(8,128)} %fusion.71) | copy-start | bytes 1572868
  237.1 68.7 %copy-start.28 = (f32[512,256]{0,1:T(8,128)S(1)}, f32[512,256]{0,1:T(8,128)}, u32[]{:S(2)}) copy-start(f32[512,256]{0,1:T(8,128)} %fusion.12) | copy-start | bytes 1572868
  531.8 45.2 %slice-start.2 = ((s8[8388608]{0:T(1024)(128)(4,1)}), s8[4194304]{0:T(1024)(128)(4,1)S(1)}, s32[]{:S(2)}) async-start(s8[8388608]{0:T(1024)(128)(4,1)} %bitcast.346), calls=%async_computation.8 | async-start | bytes 8388608
  535.6 53.5 %copy-start.1 = (f32[256,4096]{1,0:T(8,128)}, f32[256,4096]{1,0:T(8,128)S(1)}, u32[]{:S(2)}) copy-start(f32[256,4096]{1,0:T(8,128)S(1)} %convolution_subtract_fusion.4) | copy-start | bytes 12582916
  535.7 41.3 %slice-start.3 = ((s8[8388608]{0:T(1024)(128)(4,1)}), s8[4194304]{0:T(1024)(128)(4,1)S(1)}, s32[]{:S(2)}) async-start(s8[8388608]{0:T(1024)(128)(4,1)} %bitcast.346), calls=%async_computation.9 | async-start | bytes 8388608
  594.2 307.4 %all-gather.11.cloned.1.call-start = ((), (), s32[]{:S(2)}) async-start(), calls=%async_computation.3 | async-start | bytes 8912896 | tf_op jit(solution)/shard_map/all_gather | solution.py:73
  594.3 44.5 %copy-start.14 = (f32[256,256]{0,1:T(8,128)}, f32[256,256]{0,1:T(8,128)S(1)}, u32[]{:S(2)}) copy-start(f32[256,256]{0,1:T(8,128)S(1)} %negate_bitcast_fusion) | copy-start | bytes 786436
  595.2 43.5 %copy-start.4 = (f32[256,4096]{1,0:T(8,128)S(1)}, f32[256,4096]{1,0:T(8,128)}, u32[]{:S(2)}) copy-start(f32[256,4096]{1,0:T(8,128)} %copy-done.3) | copy-start | bytes 12582916
  595.2 43.5 %copy-start.29 = (f32[256,512]{1,0:T(8,128)S(1)}, f32[256,512]{1,0:T(8,128)}, u32[]{:S(2)}) copy-start(f32[256,512]{1,0:T(8,128)} %fusion.30) | copy-start | bytes 1572868
  677.3 53.5 %copy-start.25 = (f32[512]{0:T(512)S(1)}, f32[512]{0:T(512)}, u32[]{:S(2)}) copy-start(f32[512]{0:T(512)} %get-tuple-element.159) | copy-start | bytes 6148
  677.3 89.9 %copy-start.20 = (f32[256,512]{1,0:T(8,128)S(1)}, f32[256,512]{1,0:T(8,128)}, u32[]{:S(2)}) copy-start(f32[256,512]{1,0:T(8,128)} %fusion.71) | copy-start | bytes 1572868
  677.3 89.9 %copy-start.21 = (f32[256,512]{1,0:T(8,128)S(1)}, f32[256,512]{1,0:T(8,128)}, u32[]{:S(2)}) copy-start(f32[256,512]{1,0:T(8,128)} %get-tuple-element.160) | copy-start | bytes 1572868
  767.4 64.9 %slice-start.4 = ((f32[256,256]{0,1:T(8,128)}), f32[128,256]{0,1:T(8,128)S(1)}, s32[]{:S(2)}) async-start(f32[256,256]{0,1:T(8,128)} %copy-done.14), calls=%async_computation.10 | async-start | bytes 262144 | tf_op jit(solution)/shard_map/slice | solution.py:91
  769.2 129.3 %copy-start.15 = (f32[256,256]{0,1:T(8,128)S(1)}, f32[256,256]{0,1:T(8,128)}, u32[]{:S(2)}) copy-start(f32[256,256]{0,1:T(8,128)} %copy-done.14) | copy-start | bytes 786436
  769.2 66.1 %copy-start.16 = (f32[256,256]{0,1:T(8,128)S(1)}, f32[256,256]{0,1:T(8,128)}, u32[]{:S(2)}) copy-start(f32[256,256]{0,1:T(8,128)} %get-tuple-element.73) | copy-start | bytes 786436
  769.2 66.4 %copy-start.18 = (f32[256,256]{0,1:T(8,128)S(1)}, f32[256,256]{0,1:T(8,128)}, u32[]{:S(2)}) copy-start(f32[256,256]{0,1:T(8,128)} %get-tuple-element.74) | copy-start | bytes 786436
  (17 other events, 243.9 us)
Sparse Core Ops, SparseCore 0:
  13.9 66.9 all-gather.4
  83.1 62.5 all-gather.8
  232.3 92.7 all-reduce.8
  327.1 78.6 all-gather.6
  594.3 92.8 all-reduce.6
  689.2 75.9 all-gather.10
where the time goes:
time: 953 us; the launch traced here: 946 us
  matrix products  478 us (50%)
  other arithmetic  306 us (32%)
  local copies, waits for them, and re-layouts  105 us (11%)
  blocking collectives  35.8 us (4%)
  between operations  21 us (2%)
    dot_general x40, matrix products, matmul(): jnp.dot(left, right, precision=precise, preferred_element_type=jnp.float32)  408 us
    another operation x28, other arithmetic, hermitian_solve(): factor = jnp.linalg.cholesky(embedded)  139 us
    another operation x9, other arithmetic, hermitian_solve(): jax.scipy.linalg.cho_solve((factor, True), jnp.concatenate([rhs_re, rhs_i...  80.9 us
    cos x1, other arithmetic, steering(): return (jnp.cos(phase), jnp.sin(phase))  68.7 us
    slice x6, local copies, waits for them, and re-layouts, block_product(): new_re = matmul(inv_re, piece_wide[0]) - matmul(inv_im, piece_wide[1])  64 us
    dot_general x8, matrix products, tail_dot(): lax.dot_general(left, right, (((1,), (1,)), ((), ())), precision=precise,...  52.1 us
    psum x1, blocking collectives, on_device(): power = lax.psum(partial_power, 'row')  35.8 us
  transfers between devices with their start and end apart: 6, of which 0 were waited for; matrix products, arithmetic and copies ran while one was open for 82% of the time, Pallas kernels for 0%

commit v1 on v0

v1 whole, which is shorter than its diff:
```python
import functools

import jax
import jax.numpy as jnp
from jax import lax
from jax.experimental import pallas as pl
from jax.experimental.pallas import tpu as pltpu
from jax.sharding import PartitionSpec as P

f32, bf16 = jnp.float32, jnp.bfloat16
HIGHEST = lax.Precision.HIGHEST
VMEM_LIMIT = 56 * 2**20
FINE = 16


def halves(x):
    top = x.astype(bf16)
    return top, (x - top.astype(f32)).astype(bf16)


def dot1(left, right, dims=((1,), (0,))):
    return lax.dot_general(left, right, (dims, ((), ())), preferred_element_type=f32)


def dot3(left, right, dims=((1,), (0,))):
    lt, lb = halves(left)
    rt, rb = halves(right)
    return dot1(lt, rt, dims) + dot1(lt, rb, dims) + dot1(lb, rt, dims)


def dot6(left, right, dims=((1,), (0,))):
    return lax.dot_general(left, right, (dims, ((), ())), precision=HIGHEST, preferred_element_type=f32)


def cis(turns, half_turn):
    phase = jnp.pi * (turns % (2 * half_turn)).astype(f32) / half_turn
    return jnp.cos(phase), jnp.sin(phase)


def steer_kernel(blocks, low_ref, high_ref, coarse_ref, fine_ref, turn_ref, out_ref, acc, rhs_t, rhs_b):
    step = pl.program_id(0)
    rows, width = low_ref.shape[1:]
    coarse = width // FINE

    row = lax.broadcasted_iota(jnp.int32, (width, width), 0)
    col = lax.broadcasted_iota(jnp.int32, (width, width), 1)
    flip = (row + col == width - 1).astype(bf16)
    low_t, low_b = halves(jnp.concatenate([low_ref[0], low_ref[1]], 0))
    low = dot1(low_t, flip) + dot1(low_b, flip)
    high = jnp.concatenate([high_ref[0], high_ref[1]], 0)
    total, diff = high + low, high - low
    left = jnp.concatenate([total, jnp.concatenate([-diff[rows:], diff[:rows]], 0)], 1)
    left_t, left_b = halves(left)

    fine_c, fine_s = fine_ref[0], fine_ref[1]
    for q in range(coarse):
        cc, cs = coarse_ref[0, q : q + 1, :], coarse_ref[1, q : q + 1, :]
        for part, value in enumerate((cc * fine_c - cs * fine_s, cs * fine_c + cc * fine_s)):
            top, rest = halves(value)
            place = pl.ds(part * width + q * FINE, FINE)
            rhs_t[place, :] = top
            rhs_b[place, :] = rest
    top = rhs_t[...]
    term = dot1(left_t, top) + dot1(left_t, rhs_b[...]) + dot1(left_b, top)

    @pl.when(step == 0)
    def _():
        acc[...] = term

    @pl.when(step > 0)
    def _():
        acc[...] += term

    @pl.when(step == blocks - 1)
    def _():
        turn_c, turn_s = turn_ref[0:1, :], turn_ref[1:2, :]
        re, im = acc[:rows, :], acc[rows:, :]
        out_ref[0] = re * turn_c - im * turn_s
        out_ref[1] = re * turn_s + im * turn_c


def steer_product(inverse, odd):
    _, rows, length = inverse.shape
    cols = odd.shape[0]
    width = min(256, length // 2)
    blocks = length // 2 // width
    half_turn = 4 * length
    coarse = jnp.stack(cis(2 * FINE * jnp.arange(length // 2 // FINE, dtype=jnp.int32)[:, None] * odd[None, :], half_turn))
    fine = jnp.stack(cis((2 * jnp.arange(FINE, dtype=jnp.int32)[:, None] + 1) * odd[None, :], half_turn))
    turn = jnp.stack(cis((length - 1) * odd, half_turn))
    return pl.pallas_call(
        functools.partial(steer_kernel, blocks),
        grid=(blocks,),
        in_specs=[
            pl.BlockSpec((2, rows, width), lambda i: (0, 0, blocks - 1 - i)),
            pl.BlockSpec((2, rows, width), lambda i: (0, 0, blocks + i)),
            pl.BlockSpec((2, width // FINE, cols), lambda i: (0, i, 0)),
            pl.BlockSpec((2, FINE, cols), lambda i: (0, 0, 0)),
            pl.BlockSpec((2, cols), lambda i: (0, 0)),
        ],
        out_specs=pl.BlockSpec((2, rows, cols), lambda i: (0, 0, 0)),
        out_shape=jax.ShapeDtypeStruct((2, rows, cols), f32),
        scratch_shapes=[
            pltpu.VMEM((2 * rows, cols), f32),
            pltpu.VMEM((2 * width, cols), bf16),
            pltpu.VMEM((2 * width, cols), bf16),
        ],
        compiler_params=pltpu.CompilerParams(vmem_limit_bytes=VMEM_LIMIT),
        cost_estimate=pl.CostEstimate(
            flops=3 * 2 * 2 * rows * length * cols, bytes_accessed=8 * rows * length, transcendentals=0
        ),
    )(inverse, inverse, coarse, fine, turn)


def definite_inverse(matrix):
    size = matrix.shape[0]
    row = lax.broadcasted_iota(jnp.int32, (size, size), 0)
    col = lax.broadcasted_iota(jnp.int32, (size, size), 1)
    eye = (row == col).astype(f32)
    scale_c = lax.rsqrt(jnp.sum(matrix * eye, axis=1, keepdims=True))
    scale_r = lax.rsqrt(jnp.sum(matrix * eye, axis=0, keepdims=True))
    unit = matrix * scale_c * scale_r
    bound = jnp.max(jnp.sum(jnp.abs(unit), axis=0, keepdims=True))
    start = eye * (1.0 / bound)
    unit_t = unit.astype(bf16)

    def square(x):
        return jnp.sum(x * x)

    def rough_next(state):
        guess, _, last, count = state
        guess_t = guess.astype(bf16)
        residual = eye - dot1(unit_t, guess_t)
        return guess + dot1(guess_t, residual.astype(bf16)), last, square(residual), count + 1

    def rough_more(state):
        _, before, last, count = state
        return (last > 0.05) & (last < before) & (count < 16)

    big = jnp.float32(1e30)
    rough = lax.while_loop(rough_more, rough_next, (start, big * 2, big, jnp.int32(0)))[0]
    first = square(eye - dot6(unit, rough))
    guess = jnp.where(first < 0.9, rough, start)

    def fine_next(state):
        guess, _, last, count = state
        residual = eye - dot6(unit, guess)
        return guess + dot6(guess, residual), last, square(residual), count + 1

    def fine_more(state):
        _, before, last, count = state
        stalled = (last < 0.25) & (last > 0.5 * before)
        return (last > 1e-6) & jnp.logical_not(stalled) & (count < 50)

    guess = lax.while_loop(fine_more, fine_next, (guess, big * 2, big, jnp.int32(0)))[0]
    return guess * scale_c * scale_r


def finish_kernel(steps, window, length, cap_ref, cross_ref, q_ref, applied_ref, fold_ref, weights_ref, spectrum_ref, work, left):
    count = 2 * steps
    snap = cap_ref.shape[1] // count
    size = 2 * snap
    rows = q_ref.shape[1]
    lead = 2 * snap
    dirs = cross_ref.shape[2]
    eye = (
        lax.broadcasted_iota(jnp.int32, (snap, snap), 0) == lax.broadcasted_iota(jnp.int32, (snap, snap), 1)
    ).astype(f32) * window
    for i in range(count):
        up, mid, down = i * size, i * size + snap, (i + 1) * size
        for j in range(count):
            at, half, end = j * size, j * size + snap, (j + 1) * size
            re = cap_ref[0, i * snap : (i + 1) * snap, j * snap : (j + 1) * snap]
            im = cap_ref[1, i * snap : (i + 1) * snap, j * snap : (j + 1) * snap]
            if i == j:
                re = re + (eye if i % 2 == 0 else -eye)
            work[up:mid, at:half] = re
            work[up:mid, half:end] = -im
            work[mid:down, at:half] = im
            work[mid:down, half:end] = re
        re = q_ref[0, :, i * snap : (i + 1) * snap]
        im = q_ref[1, :, i * snap : (i + 1) * snap]
        left[:rows, up:mid] = re
        left[:rows, mid:down] = -im
        if i < 2:
            left[rows:, up:mid] = im
            left[rows:, mid:down] = re

    def body(k, carry):
        sign = jnp.where(k % 2 == 0, 1.0, -1.0)
        here = pl.ds(pl.multiple_of(k * size, size), size)
        pivot = definite_inverse(sign * work[here, here]) * sign
        across = dot6(pivot, work[here, :])
        work[here, :] = across
        work[here, here] = pivot

        def other(step, carry):
            i = lax.rem(k + step, count)
            there = pl.ds(pl.multiple_of(i * size, size), size)
            column = work[there, here]
            work[there, here] = jnp.zeros_like(column)
            work[there, :] -= dot6(column, work[here, :])
            return carry

        lax.fori_loop(1, count, other, 0)

        @pl.when(k == 1)
        def _():
            stacked = jnp.concatenate(
                [cross_ref[p, i * snap : (i + 1) * snap] for i in range(2) for p in range(2)], 0
            )
            solved = dot3(work[: 2 * size, : 2 * size], stacked)
            drop = jnp.sum(stacked * solved, axis=0, keepdims=True)
            moved = dot3(left[:, : 2 * size], solved)
            first = cross_ref[0, lead : lead + 1]
            second = cross_ref[1, lead : lead + 1] - drop
            first, second = length / first, length / second
            spectrum_ref[0:1] = first
            spectrum_ref[1:2] = second
            for p in range(2):
                weights_ref[0, p] = applied_ref[p, :, :dirs] * first
                weights_ref[1, p] = (applied_ref[p, :, dirs:] - moved[p * rows : (p + 1) * rows]) * second

        return carry

    lax.fori_loop(0, count, body, 0)
    fold = dot3(left[:rows], work[...])
    for i in range(count):
        fold_ref[0, :, i * snap : (i + 1) * snap] = fold[:, i * size : i * size + snap]
        fold_ref[1, :, i * snap : (i + 1) * snap] = -fold[:, i * size + snap : (i + 1) * size]


def finish(cap, cross, q, applied, steps, window, length):
    order = cap.shape[1]
    rows = q.shape[1]
    dirs = cross.shape[2]
    return pl.pallas_call(
        functools.partial(finish_kernel, steps, window, length),
        in_specs=[pl.BlockSpec(memory_space=pltpu.VMEM)] * 4,
        out_specs=[pl.BlockSpec(memory_space=pltpu.VMEM)] * 3,
        out_shape=[
            jax.ShapeDtypeStruct((2, rows, order), f32),
            jax.ShapeDtypeStruct((steps, 2, rows, dirs), f32),
            jax.ShapeDtypeStruct((steps, dirs), f32),
        ],
        scratch_shapes=[pltpu.VMEM((2 * order, 2 * order), f32), pltpu.VMEM((2 * rows, 2 * order), f32)],
        compiler_params=pltpu.CompilerParams(vmem_limit_bytes=VMEM_LIMIT),
        cost_estimate=pl.CostEstimate(flops=50 * 10**9, bytes_accessed=10**7, transcendentals=0),
    )(cap, cross, q, applied)


def update_kernel(inv_ref, fold_ref, part_ref, scale_ref, out_ref):
    rows = inv_ref.shape[1]
    scale = scale_ref[0]
    fold_re = jnp.concatenate([fold_ref[0] * scale[0:1, :], fold_ref[1] * scale[1:2, :]], 1)
    fold_im = jnp.concatenate([fold_ref[1] * scale[0:1, :], -fold_ref[0] * scale[1:2, :]], 1)
    top, rest = halves(jnp.concatenate([fold_re, fold_im], 0))
    both = part_ref[...]
    low = (both << 16) >> 16
    value = jnp.concatenate([(both - low) >> 16, low], 1)
    upper = (value + 128) >> 8
    lower = (value - upper * 256).astype(f32).astype(bf16)
    upper = (upper * 256).astype(f32).astype(bf16)
    dims = ((1,), (1,))
    change = dot1(top, upper, dims) + dot1(rest, upper, dims) + dot1(top, lower, dims)
    out_ref[0] = inv_ref[0] - change[:rows]
    out_ref[1] = inv_ref[1] - change[rows:]


def low_rank_update(inverse, fold, parts, scales):
    _, rows, length = inverse.shape
    order = fold.shape[2]
    return pl.pallas_call(
        update_kernel,
        grid=(length // rows,),
        in_specs=[
            pl.BlockSpec((2, rows, rows), lambda i: (0, 0, i)),
            pl.BlockSpec((2, rows, order), lambda i: (0, 0, 0)),
            pl.BlockSpec((rows, order), lambda i: (i, 0)),
            pl.BlockSpec((1, 2, order), lambda i: (i, 0, 0)),
        ],
        out_specs=pl.BlockSpec((2, rows, rows), lambda i: (0, 0, i)),
        out_shape=jax.ShapeDtypeStruct(inverse.shape, f32),
        compiler_params=pltpu.CompilerParams(vmem_limit_bytes=VMEM_LIMIT),
        cost_estimate=pl.CostEstimate(
            flops=24 * rows * order * length, bytes_accessed=16 * rows * length, transcendentals=0
        ),
    )(inverse, fold, parts, scales)


def product_kernel(blocks, lead, inv_ref, all_ref, snaps_ref, applied_ref, coarse_ref, fine_ref,
                   q_ref, cap_ref, cross_ref, parts_ref, scale_ref, acc, steer):
    step = pl.program_id(0)
    rows = inv_ref.shape[1]
    order = snaps_ref.shape[2]
    left = jnp.concatenate(halves(jnp.concatenate([inv_ref[0], inv_ref[1]], 0)), 0)
    term = dot1(left, jnp.concatenate([all_ref[0], all_ref[1]], 1))

    @pl.when(step == 0)
    def _():
        acc[...] = term

    @pl.when(step > 0)
    def _():
        acc[...] += term

    @pl.when(step == blocks - 1)
    def _():
        total = acc[: 2 * rows] + acc[2 * rows :]
        re = total[:rows, :order] - total[rows:, order:]
        im = total[:rows, order:] + total[rows:, :order]
        q_ref[0] = re
        q_ref[1] = im
        packed = 0
        for part, value in enumerate((re, im)):
            peak = jnp.max(jnp.abs(value), axis=0, keepdims=True)
            scale = jnp.where(peak > 0, peak, 1.0) / 32767.0
            scale_ref[0, part : part + 1] = scale
            whole = jnp.clip(jnp.round(value / scale), -32767, 32767).astype(jnp.int32)
            packed = packed * 65536 + whole
        parts_ref[...] = packed

        dims = ((0,), (0,))
        both = jnp.concatenate([re, im], 1)
        snaps = jnp.concatenate([snaps_ref[0], snaps_ref[1]], 1)
        top = both.astype(bf16)
        mid, low = halves(both - top.astype(f32))
        sums = dot1(snaps, top, dims) + dot1(snaps, mid, dims) + dot1(snaps, low, dims)
        cap_ref[0] = sums[:order, :order] + sums[order:, order:]
        cap_ref[1] = sums[:order, order:] - sums[order:, :order]

        cols = steer.shape[2]
        dirs = cols // 2
        fine_c, fine_s = fine_ref[0], fine_ref[1]
        for g in range(rows // FINE):
            cc, cs = coarse_ref[0, g : g + 1, :], coarse_ref[1, g : g + 1, :]
            steer[0, g * FINE : (g + 1) * FINE, :] = cc * fine_c - cs * fine_s
            steer[1, g * FINE : (g + 1) * FINE, :] = cs * fine_c + cc * fine_s
        power = jnp.sum(steer[0] * applied_ref[0] + steer[1] * applied_ref[1], axis=0, keepdims=True)
        first = jnp.concatenate([re[:, :lead], im[:, :lead]], 1)
        later = jnp.concatenate([steer[0, :, dirs:], steer[1, :, dirs:]], 1)
        sums = dot3(first, later, dims)
        cross_ref[0, :lead] = sums[:lead, :dirs] + sums[lead:, dirs:]
        cross_ref[1, :lead] = sums[:lead, dirs:] - sums[lead:, :dirs]
        extra = cross_ref.shape[1] - lead
        cross_ref[0, lead:] = jnp.broadcast_to(power[:, :dirs], (extra, dirs))
        cross_ref[1, lead:] = jnp.broadcast_to(power[:, dirs:], (extra, dirs))


def product(inverse, snaps_all, snaps, applied, coarse, fine, lead):
    _, rows, length = inverse.shape
    order = snaps.shape[2]
    cols = applied.shape[2]
    width = min(512, length)
    blocks = length // width
    keep = lambda *shape: pl.BlockSpec(shape, lambda i: (0,) * len(shape))
    shapes = [
        ((2, rows, order), f32),
        ((2, order, order), f32),
        ((2, lead + 8, cols // 2), f32),
        ((rows, order), jnp.int32),
        ((1, 2, order), f32),
    ]
    return pl.pallas_call(
        functools.partial(product_kernel, blocks, lead),
        grid=(blocks,),
        in_specs=[
            pl.BlockSpec((2, rows, width), lambda i: (0, 0, i)),
            pl.BlockSpec((2, width, order), lambda i: (0, i, 0)),
            keep(*snaps.shape),
            keep(*applied.shape),
            keep(*coarse.shape),
            keep(*fine.shape),
        ],
        out_specs=[keep(*shape) for shape, _ in shapes],
        out_shape=[jax.ShapeDtypeStruct(shape, kind) for shape, kind in shapes],
        scratch_shapes=[pltpu.VMEM((4 * rows, 2 * order), f32), pltpu.VMEM((2, rows, cols), f32)],
        compiler_params=pltpu.CompilerParams(vmem_limit_bytes=VMEM_LIMIT),
        cost_estimate=pl.CostEstimate(
            flops=16 * rows * length * order, bytes_accessed=16 * rows * length, transcendentals=0
        ),
    )(inverse, snaps_all, snaps, applied, coarse, fine)


def on_device(inverse, cycle, arrivals, departing, directions):
    _, rows, length = inverse.shape
    window = cycle.shape[2]
    steps, _, _, snap = arrivals.shape
    dirs = directions.shape[1]

    slots = lax.broadcasted_iota(jnp.int32, (window, steps * snap), 0)
    pick = (slots == departing.reshape(1, -1)).astype(bf16)
    departed = dot1(cycle.reshape(2 * rows, window), pick).astype(bf16).reshape(2, rows, steps, snap)
    snaps = jnp.concatenate([jnp.moveaxis(arrivals, 0, 2), departed], axis=3).reshape(2, rows, 2 * steps * snap)
    snaps_all = lax.all_gather(snaps, "row", axis=1, tiled=True)

    odd = (2 * directions + 1 - 2 * length).reshape(-1)
    applied = steer_product(inverse, odd)

    first_row = lax.axis_index("row") * rows
    coarse = jnp.stack(
        cis((first_row + FINE * jnp.arange(rows // FINE, dtype=jnp.int32))[:, None] * odd[None, :], 2 * length)
    )
    fine = jnp.stack(cis(jnp.arange(FINE, dtype=jnp.int32)[:, None] * odd[None, :], 2 * length))
    q, cap, cross, parts, scale = product(inverse, snaps_all, snaps, applied, coarse, fine, 2 * snap)
    cap, cross = lax.psum((cap, cross), "row")
    parts_all = lax.all_gather(parts, "row", axis=0, tiled=True)
    scales_all = lax.all_gather(scale, "row", axis=0, tiled=True)

    fold, weights, spectrum = finish(cap, cross, q, applied, steps, window, length)
    new_inverse = low_rank_update(inverse, fold, parts_all, scales_all)
    return new_inverse, weights, spectrum


def solution(mesh):
    in_specs = (
        P("groups", "row", None),
        P("groups", "row", None),
        P("groups", None, "row", None),
        P("groups", None),
        P("groups", None),
    )
    out_specs = (P("groups", "row", None), P("groups", None, "row", None), P("groups", None))
    return jax.shard_map(
        on_device, mesh=mesh, in_specs=in_specs, out_specs=out_specs, check_vma=False
    )
```

time: 953 us -> 319 us (0.33)
  matrix products: 478 us -> 1.17 us
  other arithmetic: 306 us -> 6.21 us
  waiting for transfers between devices: 0.19 us -> 160 us
  Pallas kernels: 0 us -> 114 us
  local copies, waits for them, and re-layouts: 105 us -> 2.39 us
  blocking collectives: 35.8 us -> 20.9 us
    dot_general x56 -> x1, matrix products: 465 us -> 1.17 us  [dot1(): lax.dot_general(left, right, (dims, ((), ())), preferred_element_type=f32)]
    another operation x46 -> x4, other arithmetic: 228 us -> 3.08 us  [the longest x1 1.09 us: steer_product(): jnp.stack(cis(2 * FINE * jnp.arange(length // 2 // FINE, dtype=jnp.int32)...]
    pallas_call x0 -> x4, Pallas kernels: none -> 114 us  [the longest x1 48.3 us: finish(): pl.pallas_call(functools.partial(finish_kernel, steps, window, length), i...]
    psum x2 -> x1, waiting for transfers between devices: 0.01 us -> 81.1 us  [on_device(): cap, cross = lax.psum((cap, cross), 'row')]
    all_gather x4 -> x2, waiting for transfers between devices: 0.08 us -> 78.3 us  [the longest x1 50.2 us: on_device(): snaps_all = lax.all_gather(snaps, 'row', axis=1, tiled=True)]
    slice x18 -> x0, local copies, waits for them, and re-layouts: 68.1 us -> none  [the longest x6 64 us: block_product(): new_re = matmul(inv_re, piece_wide[0]) - matmul(inv_im, piece_wide[1])]
    cos x1 -> x3, other arithmetic: 68.7 us -> 3.05 us  [cis(): return (jnp.cos(phase), jnp.sin(phase))]
    psum x1 -> x0, blocking collectives: 35.8 us -> none  [on_device(): power = lax.psum(partial_power, 'row')]
  transfers between devices with their start and end apart: 6 -> 3, of which waited for: 0 -> 3; matrix products, arithmetic and copies ran while one was open for 82% -> 2% of each run, Pallas kernels for 0% -> 22%
where the time goes in v1:
time: 319 us
  waiting for transfers between devices  160 us (50%)
  Pallas kernels  114 us (36%)
  blocking collectives  20.9 us (7%)
  between operations  13.9 us (4%)
  other arithmetic  6.21 us (2%)
    psum x1, waiting for transfers between devices, on_device(): cap, cross = lax.psum((cap, cross), 'row')  81.1 us
    all_gather x1, waiting for transfers between devices, on_device(): snaps_all = lax.all_gather(snaps, 'row', axis=1, tiled=True)  50.2 us
    pallas_call x1, Pallas kernels, finish(): pl.pallas_call(functools.partial(finish_kernel, steps, window, length), i...  48.3 us
    all_gather x1, waiting for transfers between devices, on_device(): parts_all = lax.all_gather(parts, 'row', axis=0, tiled=True)  28.2 us
    pallas_call x1, Pallas kernels, low_rank_update(): pl.pallas_call(update_kernel, grid=(length // rows,), in_specs=[pl.BlockS...  22.9 us
    pallas_call x1, Pallas kernels, product(): pl.pallas_call(functools.partial(product_kernel, blocks, lead), grid=(blo...  21.2 us
    pallas_call x1, Pallas kernels, steer_product(): pl.pallas_call(functools.partial(steer_kernel, blocks), grid=(blocks,), i...  21.2 us
    all_gather x1, blocking collectives, on_device(): scales_all = lax.all_gather(scale, 'row', axis=0, tiled=True)  20.9 us
  transfers between devices with their start and end apart: 3, of which 3 were waited for; matrix products, arithmetic and copies ran while one was open for 2% of the time, Pallas kernels for 22%

profile of v1, /device:TPU:0, one launch (start us, length us, event | category | flops | bytes accessed | tf_op | source)
XLA Modules:
  0.0 318.5 jit_solution(15107299997266965285)
XLA Ops:
  7.2 1.2 copy-done
  8.4 1.2 fusion
  9.6 0.1 reshape.605
  9.7 0.2 copy.10
  9.9 0.1 maximum_bitcast_fusion
  9.9 0.8 copy.12
  10.8 0.0 all-reduce.3.cloned.1.call-start
  10.9 0.1 fusion.31
  11.0 0.1 sin.52
  11.2 0.6 pad_maximum_fusion.4.turn_ref
  11.8 0.8 fusion.22
  12.6 0.7 pad_maximum_fusion.3.fine_ref
  13.3 0.7 pad_maximum_fusion.1
  14.0 2.1 fusion.8
  16.1 1.1 pad_maximum_fusion.coarse_ref
  17.2 21.2 %shard_map.76.applied_ref = f32[2,256,1024]{2,1,0:T(8,128)} custom-call(f32[2,256,4096]{2,1,0:T(8,128)} %inv_ref.3, f32[2,256,4096]{2,1,0:T(8,128)} %inv_ref.3, f32[2,128,1024]{2,1,0:T(8,128)} %pad_maximum_fusion.coarse_ref, f32[2,16,1024]{2,1,0:T(8,128)} %get-tuple-element.37.fine_ref, f32[2,1024]{1,0:T(2,128)} %pad_maximum_fusion.4.turn_ref), custom_call_target="tpu_custom_call" | custom-call | flops 12884901888 | bytes 8388608 | tf_op jit(solution)/shard_map/pallas_call | solution.py:91
  38.4 50.2 %all-gather.3.cloned.1.call-done.all_ref = bf16[2,4096,512]{2,1,0:T(8,128)(2,1)} async-done(((bf16[2,256,512]{2,1,0:T(8,128)(2,1)}), bf16[2,4096,512]{2,1,0:T(8,128)(2,1)}) %all-gather.3.cloned.1.call-update) | async-done | bytes 8388624 | tf_op jit(solution)/shard_map/all_gather | solution.py:395
  88.6 21.2 %shard_map.77 = (f32[2,256,512]{2,1,0:T(8,128)}, f32[2,512,512]{2,1,0:T(8,128)}, f32[2,264,512]{2,1,0:T(8,128)}, s32[256,512]{1,0:T(8,128)}, f32[1,2,512]{2,1,0:T(2,128)}) custom-call(f32[2,256,4096]{2,1,0:T(8,128)} %inv_ref.3, bf16[2,4096,512]{2,1,0:T(8,128)(2,1)} %all-gather.3.cloned.1.call-done.all_ref, bf16[2,256,512]{2,1,0:T(8,128)(2,1)} %bitcast.20, ...), custom_call_target="tpu_custom_call" | custom-call | flops 8589934592 | bytes 16777216 | tf_op jit(solution)/shard_map/pallas_call | solution.py:364
  109.9 0.7 all-gather.5.cloned.1.call-update
  110.6 20.9 %all_gather.11.scale_ref = f32[16,2,512]{2,1,0:T(2,128)} all-gather(f32[1,2,512]{2,1,0:T(2,128)S(1)} %copy-done.3), channel_id=1, replica_groups=mesh['groups'=2,'row'=16] {'row'}, dimensions={0}, use_global_device_ids=true | all-gather | bytes 69632 | tf_op jit(solution)/shard_map/all_gather | solution.py:408
  131.5 81.1 %all-reduce.3.cloned.1.call-done = (f32[2,512,512]{2,1,0:T(8,128)}, f32[2,264,512]{2,1,0:T(8,128)}) async-done(((f32[2,512,512]{2,1,0:T(8,128)}, f32[2,264,512]{2,1,0:T(8,128)}), (f32[2,512,512]{2,1,0:T(8,128)}, f32[2,264,512]{2,1,0:T(8,128)})) %all-reduce.3.cloned.1.call-update) | async-done | bytes 3178512 | tf_op jit(solution)/shard_map/psum | solution.py:406
  212.6 48.3 %shard_map.78 = (f32[2,256,512]{2,1,0:T(8,128)}, f32[2,2,256,512]{3,2,1,0:T(8,128)}, f32[2,512]{1,0:T(2,128)}) custom-call(f32[2,512,512]{2,1,0:T(8,128)} %get-tuple-element.19.cap_ref, f32[2,264,512]{2,1,0:T(8,128)} %get-tuple-element.20.cross_ref, f32[2,256,512]{2,1,0:T(8,128)} %get-tuple-element.13.q_ref, f32[2,256,1024]{2,1,0:T(8,128)} %shard_map.76.applied_ref), custom_call_target="tpu_custom_call" | custom-call | flops 49999998976 | bytes 10000000 | tf_op jit(solution)/shard_map/pallas_call | solution.py:237
  260.9 28.2 %all-gather.5.cloned.1.call-done.part_ref = s32[4096,512]{1,0:T(8,128)} async-done(((s32[256,512]{1,0:T(8,128)}), s32[4096,512]{1,0:T(8,128)}) %all-gather.5.cloned.1.call-update) | async-done | bytes 8388624 | tf_op jit(solution)/shard_map/all_gather | solution.py:407
  289.1 22.9 %shard_map.79 = f32[2,256,4096]{2,1,0:T(8,128)} custom-call(f32[2,256,4096]{2,1,0:T(8,128)} %inv_ref.3, f32[2,256,512]{2,1,0:T(8,128)} %get-tuple-element.14.fold_ref, s32[4096,512]{1,0:T(8,128)} %all-gather.5.cloned.1.call-done.part_ref, f32[16,2,512]{2,1,0:T(2,128)} %all_gather.11.scale_ref), custom_call_target="tpu_custom_call" | custom-call | flops 12884901888 | bytes 16777216 | tf_op jit(solution)/shard_map/pallas_call | solution.py:273
  (17 shorter events, 0.2 us)
Async XLA Ops:
  7.2 1.2 copy-start
  7.2 2.7 copy-start.1
  7.2 81.4 %all-gather.3.cloned.1.call-start = ((), (), s32[]{:S(2)}) async-start(), calls=%async_computation | async-start | bytes 8912896 | tf_op jit(solution)/shard_map/all_gather | solution.py:395
  9.6 1.3 copy-start.2
  10.8 201.8 %all-reduce.3.cloned.1.call-start = ((), (), s32[]{:S(2)}) async-start(), calls=%async_computation.2 | async-start | bytes 6356992 | tf_op jit(solution)/shard_map/psum | solution.py:406
  109.8 0.8 copy-start.3
  109.8 179.3 %all-gather.5.cloned.1.call-start = ((), (), s32[]{:S(2)}) async-start(), calls=%async_computation.1 | async-start | bytes 8912896 | tf_op jit(solution)/shard_map/all_gather | solution.py:407
Sparse Core Ops, SparseCore 0:
  10.9 77.6 all-gather.2
  109.9 102.5 all-reduce.2
  215.0 74.0 all-gather.4

commit v2 on v1

--- a/solution.py
+++ b/solution.py
@@ -35,6 +35,104 @@
 def cis(turns, half_turn):
     phase = jnp.pi * (turns % (2 * half_turn)).astype(f32) / half_turn
     return jnp.cos(phase), jnp.sin(phase)
+
+
+TAIL = 16
+
+
+def ring_place(chip, chips):
+    odd = chip % 2
+    return (1 - odd) * (chip // 2) + odd * (chips - 1 - chip // 2)
+
+
+def ring_chip(place, chips):
+    back = place // (chips // 2)
+    return (1 - back) * 2 * place + back * (2 * (chips - place) - 1)
+
+
+def gather_kernel(chips, x_ref, out_ref, own_sem, up_send, up_recv, down_send, down_recv, pair_send, pair_recv):
+    me = lax.axis_index("row")
+    core = me % 2
+    place = ring_place(me // 2, chips)
+    pair = me + 1 - 2 * core
+    above = ring_chip((place + 1) % chips, chips) * 2 + core
+    below = ring_chip((place + chips - 1) % chips, chips) * 2 + core
+    mesh_id = pl.DeviceIdType.MESH
+    half = x_ref.shape[0] // 2
+    steps = chips // 2
+
+    barrier = pltpu.get_barrier_semaphore()
+    for device in (above, below, pair):
+        pl.semaphore_signal(barrier, inc=1, device_id={"row": device}, device_id_type=mesh_id)
+    pl.semaphore_wait(barrier, 3)
+
+    def block(offset):
+        return ring_chip((place + offset + chips) % chips, chips) * 2 + core
+
+    def send(source, target, device, send_sem, recv_sem):
+        copy = pltpu.make_async_remote_copy(
+            src_ref=source, dst_ref=target, send_sem=send_sem, recv_sem=recv_sem,
+            device_id={"row": device}, device_id_type=mesh_id,
+        )
+        copy.start()
+        return copy
+
+    own = pltpu.make_async_copy(x_ref, out_ref.at[me], own_sem)
+    own.start()
+    pairs = [send(x_ref, out_ref.at[me], pair, pair_send.at[0], pair_recv.at[0])]
+    sent = []
+    for t in range(steps):
+        up, down = block(-t), block(t)
+        last = t == steps - 1
+        rows_up = pl.ds(0, half) if last else pl.ds(0, 2 * half)
+        rows_down = pl.ds(half, half) if last else pl.ds(0, 2 * half)
+        from_up = x_ref if t == 0 else out_ref.at[up]
+        from_down = x_ref if t == 0 else out_ref.at[down]
+        moving = (
+            send(from_up.at[rows_up], out_ref.at[up, rows_up], above, up_send.at[t], up_recv.at[t]),
+            send(from_down.at[rows_down], out_ref.at[down, rows_down], below, down_send.at[t], down_recv.at[t]),
+        )
+        sent.extend(moving)
+        for copy, offset, rows in zip(moving, (-t - 1, t + 1), (rows_up, rows_down)):
+            copy.wait_recv()
+            here = out_ref.at[block(offset), rows]
+            spot = len(pairs)
+            pairs.append(send(here, here, pair, pair_send.at[spot], pair_recv.at[spot]))
+    for copy in sent:
+        copy.wait_send()
+    for copy in pairs:
+        copy.wait()
+    own.wait()
+
+
+def gather(x, devices, collective_id):
+    chips = devices // 2
+    steps = chips // 2
+    dma = pltpu.SemaphoreType.DMA
+    return pl.pallas_call(
+        functools.partial(gather_kernel, chips),
+        in_specs=[pl.BlockSpec(memory_space=pl.ANY)],
+        out_specs=pl.BlockSpec(memory_space=pl.ANY),
+        out_shape=jax.ShapeDtypeStruct((devices,) + x.shape, x.dtype),
+        scratch_shapes=[dma] + [dma((steps,))] * 4 + [dma((2 * steps + 1,))] * 2,
+        compiler_params=pltpu.CompilerParams(collective_id=collective_id, has_side_effects=True),
+        cost_estimate=pl.CostEstimate(flops=0, bytes_accessed=2 * devices * x.size * x.dtype.itemsize, transcendentals=0),
+    )(x)
+
+
+def power_of_two(peak, most):
+    ratio = jnp.where(peak > 0, peak, 1.0) / most
+    return jnp.clip(jnp.ceil(jnp.log2(ratio)), -120, 120).astype(jnp.int32)
+
+
+def unpack(packed):
+    low = (packed << 16) >> 16
+    return (packed - low) >> 16, low
+
+
+def pieces(whole):
+    upper = (whole + 128) >> 8
+    return (upper * 256).astype(f32).astype(bf16), (whole - upper * 256).astype(f32).astype(bf16)
 
 
 def steer_kernel(blocks, low_ref, high_ref, coarse_ref, fine_ref, turn_ref, out_ref, acc, rhs_t, rhs_b):
@@ -249,25 +347,20 @@
     )(cap, cross, q, applied)
 
 
-def update_kernel(inv_ref, fold_ref, part_ref, scale_ref, out_ref):
+def update_kernel(inv_ref, fold_ref, part_ref, out_ref):
     rows = inv_ref.shape[1]
-    scale = scale_ref[0]
+    scale = jnp.exp2(part_ref[0, rows : rows + 2].astype(f32))
     fold_re = jnp.concatenate([fold_ref[0] * scale[0:1, :], fold_ref[1] * scale[1:2, :]], 1)
     fold_im = jnp.concatenate([fold_ref[1] * scale[0:1, :], -fold_ref[0] * scale[1:2, :]], 1)
     top, rest = halves(jnp.concatenate([fold_re, fold_im], 0))
-    both = part_ref[...]
-    low = (both << 16) >> 16
-    value = jnp.concatenate([(both - low) >> 16, low], 1)
-    upper = (value + 128) >> 8
-    lower = (value - upper * 256).astype(f32).astype(bf16)
-    upper = (upper * 256).astype(f32).astype(bf16)
+    upper, lower = pieces(jnp.concatenate(unpack(part_ref[0, :rows]), 1))
     dims = ((1,), (1,))
     change = dot1(top, upper, dims) + dot1(rest, upper, dims) + dot1(top, lower, dims)
     out_ref[0] = inv_ref[0] - change[:rows]
     out_ref[1] = inv_ref[1] - change[rows:]
 
 
-def low_rank_update(inverse, fold, parts, scales):
+def low_rank_update(inverse, fold, parts_all):
     _, rows, length = inverse.shape
     order = fold.shape[2]
     return pl.pallas_call(
@@ -276,8 +369,7 @@
         in_specs=[
             pl.BlockSpec((2, rows, rows), lambda i: (0, 0, i)),
             pl.BlockSpec((2, rows, order), lambda i: (0, 0, 0)),
-            pl.BlockSpec((rows, order), lambda i: (i, 0)),
-            pl.BlockSpec((1, 2, order), lambda i: (i, 0, 0)),
+            pl.BlockSpec((1, rows + TAIL, order), lambda i: (i, 0, 0)),
         ],
         out_specs=pl.BlockSpec((2, rows, rows), lambda i: (0, 0, i)),
         out_shape=jax.ShapeDtypeStruct(inverse.shape, f32),
@@ -285,16 +377,18 @@
         cost_estimate=pl.CostEstimate(
             flops=24 * rows * order * length, bytes_accessed=16 * rows * length, transcendentals=0
         ),
-    )(inverse, fold, parts, scales)
-
-
-def product_kernel(blocks, lead, inv_ref, all_ref, snaps_ref, applied_ref, coarse_ref, fine_ref,
-                   q_ref, cap_ref, cross_ref, parts_ref, scale_ref, acc, steer):
+    )(inverse, fold, parts_all)
+
+
+def product_kernel(blocks, inv_ref, all_ref, applied_ref, coarse_ref, fine_ref, q_ref, parts_ref, acc, steer):
     step = pl.program_id(0)
     rows = inv_ref.shape[1]
-    order = snaps_ref.shape[2]
+    order = all_ref.shape[2]
     left = jnp.concatenate(halves(jnp.concatenate([inv_ref[0], inv_ref[1]], 0)), 0)
-    term = dot1(left, jnp.concatenate([all_ref[0], all_ref[1]], 1))
+    right = jnp.concatenate(
+        [jnp.concatenate([all_ref[i, :rows], all_ref[i, rows:]], 1) for i in range(all_ref.shape[0])], 0
+    )
+    term = dot1(left, right)
 
     @pl.when(step == 0)
     def _():
@@ -311,23 +405,14 @@
         im = total[:rows, order:] + total[rows:, :order]
         q_ref[0] = re
         q_ref[1] = im
+        parts_ref[rows:] = jnp.zeros((TAIL, order), jnp.int32)
         packed = 0
         for part, value in enumerate((re, im)):
-            peak = jnp.max(jnp.abs(value), axis=0, keepdims=True)
-            scale = jnp.where(peak > 0, peak, 1.0) / 32767.0
-            scale_ref[0, part : part + 1] = scale
-            whole = jnp.clip(jnp.round(value / scale), -32767, 32767).astype(jnp.int32)
-            packed = packed * 65536 + whole
-        parts_ref[...] = packed
-
-        dims = ((0,), (0,))
-        both = jnp.concatenate([re, im], 1)
-        snaps = jnp.concatenate([snaps_ref[0], snaps_ref[1]], 1)
-        top = both.astype(bf16)
-        mid, low = halves(both - top.astype(f32))
-        sums = dot1(snaps, top, dims) + dot1(snaps, mid, dims) + dot1(snaps, low, dims)
-        cap_ref[0] = sums[:order, :order] + sums[order:, order:]
-        cap_ref[1] = sums[:order, order:] - sums[order:, :order]
+            power = power_of_two(jnp.max(jnp.abs(value), axis=0, keepdims=True), 32767.0)
+            parts_ref[rows + part : rows + part + 1] = power
+            whole = jnp.round(value / jnp.exp2(power.astype(f32)))
+            packed = packed * 65536 + jnp.clip(whole, -32767, 32767).astype(jnp.int32)
+        parts_ref[:rows] = packed
 
         cols = steer.shape[2]
         dirs = cols // 2
@@ -336,38 +421,28 @@
             cc, cs = coarse_ref[0, g : g + 1, :], coarse_ref[1, g : g + 1, :]
             steer[0, g * FINE : (g + 1) * FINE, :] = cc * fine_c - cs * fine_s
             steer[1, g * FINE : (g + 1) * FINE, :] = cs * fine_c + cc * fine_s
-        power = jnp.sum(steer[0] * applied_ref[0] + steer[1] * applied_ref[1], axis=0, keepdims=True)
-        first = jnp.concatenate([re[:, :lead], im[:, :lead]], 1)
-        later = jnp.concatenate([steer[0, :, dirs:], steer[1, :, dirs:]], 1)
-        sums = dot3(first, later, dims)
-        cross_ref[0, :lead] = sums[:lead, :dirs] + sums[lead:, dirs:]
-        cross_ref[1, :lead] = sums[:lead, dirs:] - sums[lead:, :dirs]
-        extra = cross_ref.shape[1] - lead
-        cross_ref[0, lead:] = jnp.broadcast_to(power[:, :dirs], (extra, dirs))
-        cross_ref[1, lead:] = jnp.broadcast_to(power[:, dirs:], (extra, dirs))
-
-
-def product(inverse, snaps_all, snaps, applied, coarse, fine, lead):
+        sums = jnp.sum(steer[0] * applied_ref[0] + steer[1] * applied_ref[1], axis=0, keepdims=True)
+        power = power_of_two(jnp.max(jnp.abs(sums), axis=1, keepdims=True), 2.0**30)
+        whole = jnp.round(sums / jnp.exp2(power.astype(f32))).astype(jnp.int32)
+        parts_ref[rows + 2 : rows + 3, :dirs] = whole[:, :dirs]
+        parts_ref[rows + 3 : rows + 4, :dirs] = whole[:, dirs:]
+        parts_ref[rows + 4 : rows + 5, :dirs] = jnp.broadcast_to(power, (1, dirs))
+
+
+def product(inverse, snaps_all, applied, coarse, fine):
     _, rows, length = inverse.shape
-    order = snaps.shape[2]
+    order = snaps_all.shape[2]
     cols = applied.shape[2]
-    width = min(512, length)
-    blocks = length // width
+    group = 2
+    blocks = length // rows // group
     keep = lambda *shape: pl.BlockSpec(shape, lambda i: (0,) * len(shape))
-    shapes = [
-        ((2, rows, order), f32),
-        ((2, order, order), f32),
-        ((2, lead + 8, cols // 2), f32),
-        ((rows, order), jnp.int32),
-        ((1, 2, order), f32),
-    ]
+    shapes = [((2, rows, order), f32), ((rows + TAIL, order), jnp.int32)]
     return pl.pallas_call(
-        functools.partial(product_kernel, blocks, lead),
+        functools.partial(product_kernel, blocks),
         grid=(blocks,),
         in_specs=[
-            pl.BlockSpec((2, rows, width), lambda i: (0, 0, i)),
-            pl.BlockSpec((2, width, order), lambda i: (0, i, 0)),
-            keep(*snaps.shape),
+            pl.BlockSpec((2, rows, group * rows), lambda i: (0, 0, i)),
+            pl.BlockSpec((group, 2 * rows, order), lambda i: (i, 0, 0)),
             keep(*applied.shape),
             keep(*coarse.shape),
             keep(*fine.shape),
@@ -379,7 +454,60 @@
         cost_estimate=pl.CostEstimate(
             flops=16 * rows * length * order, bytes_accessed=16 * rows * length, transcendentals=0
         ),
-    )(inverse, snaps_all, snaps, applied, coarse, fine)
+    )(inverse, snaps_all, applied, coarse, fine)
+
+
+def sums_kernel(blocks, parts_ref, snaps_ref, cap_ref, power_ref, acc, powers):
+    step = pl.program_id(0)
+    rows = snaps_ref.shape[1] // 2
+    order = snaps_ref.shape[2]
+    dirs = power_ref.shape[2]
+
+    @pl.when(step == 0)
+    def _():
+        acc[...] = jnp.zeros_like(acc)
+        powers[...] = jnp.zeros_like(powers)
+
+    dims = ((0,), (0,))
+    re, im = unpack(parts_ref[0, :rows])
+    scales = jnp.exp2(parts_ref[0, rows : rows + 2].astype(f32))
+    snaps = jnp.concatenate([snaps_ref[0, :rows], snaps_ref[0, rows:]], 1)
+    upper, lower = pieces(jnp.concatenate([re, im], 1))
+    scale = jnp.concatenate([scales[0:1], scales[1:2]], 1)
+    acc[...] += (dot1(snaps, upper, dims) + dot1(snaps, lower, dims)) * scale
+
+    unit = jnp.exp2(parts_ref[0, rows + 4 : rows + 5, :dirs].astype(f32))
+    powers[0:1] += parts_ref[0, rows + 2 : rows + 3, :dirs].astype(f32) * unit
+    powers[1:2] += parts_ref[0, rows + 3 : rows + 4, :dirs].astype(f32) * unit
+
+    @pl.when(step == blocks - 1)
+    def _():
+        cap_ref[0] = acc[:order, :order] + acc[order:, order:]
+        cap_ref[1] = acc[:order, order:] - acc[order:, :order]
+        power_ref[0] = jnp.broadcast_to(powers[0:1], (8, dirs))
+        power_ref[1] = jnp.broadcast_to(powers[1:2], (8, dirs))
+
+
+def sums(parts_all, snaps_all, dirs):
+    blocks, packed, order = parts_all.shape
+    rows = packed - TAIL
+    keep = lambda *shape: pl.BlockSpec(shape, lambda i: (0,) * len(shape))
+    shapes = [(2, order, order), (2, 8, dirs)]
+    return pl.pallas_call(
+        functools.partial(sums_kernel, blocks),
+        grid=(blocks,),
+        in_specs=[
+            pl.BlockSpec((1, packed, order), lambda i: (i, 0, 0)),
+            pl.BlockSpec((1, 2 * rows, order), lambda i: (i, 0, 0)),
+        ],
+        out_specs=[keep(*shape) for shape in shapes],
+        out_shape=[jax.ShapeDtypeStruct(shape, f32) for shape in shapes],
+        scratch_shapes=[
+            pltpu.VMEM((2 * order, 2 * order), f32),
+            pltpu.VMEM((8, dirs), f32),
+        ],
+        compiler_params=pltpu.CompilerParams(vmem_limit_bytes=VMEM_LIMIT),
+    )(parts_all, snaps_all)
 
 
 def on_device(inverse, cycle, arrivals, departing, directions):
@@ -391,24 +519,42 @@
     slots = lax.broadcasted_iota(jnp.int32, (window, steps * snap), 0)
     pick = (slots == departing.reshape(1, -1)).astype(bf16)
     departed = dot1(cycle.reshape(2 * rows, window), pick).astype(bf16).reshape(2, rows, steps, snap)
-    snaps = jnp.concatenate([jnp.moveaxis(arrivals, 0, 2), departed], axis=3).reshape(2, rows, 2 * steps * snap)
-    snaps_all = lax.all_gather(snaps, "row", axis=1, tiled=True)
+    snaps = jnp.concatenate([jnp.moveaxis(arrivals, 0, 2), departed], axis=3).reshape(2 * rows, 2 * steps * snap)
+    devices = length // rows
+    snaps_all = gather(snaps, devices, 0)
 
     odd = (2 * directions + 1 - 2 * length).reshape(-1)
     applied = steer_product(inverse, odd)
 
-    first_row = lax.axis_index("row") * rows
-    coarse = jnp.stack(
-        cis((first_row + FINE * jnp.arange(rows // FINE, dtype=jnp.int32))[:, None] * odd[None, :], 2 * length)
+    coarse = jnp.stack(cis(FINE * jnp.arange(length // FINE, dtype=jnp.int32)[:, None] * odd[None, :], 2 * length))
+    fine = jnp.stack(cis(jnp.arange(FINE, dtype=jnp.int32)[:, None] * odd[None, :], 2 * length))
+    first = lax.axis_index("row") * (rows // FINE)
+    local = lax.dynamic_slice_in_dim(coarse, first, rows // FINE, 1)
+    q, parts = product(inverse, snaps_all, applied, local, fine)
+    parts_all = gather(parts, devices, 1)
+    cap, power = sums(parts_all, snaps_all, dirs)
+
+    lead = 2 * snap
+    scales = jnp.exp2(parts_all[:, rows : rows + 2, :lead].astype(f32))
+    parts_re, parts_im = unpack(parts_all[:, :rows, :lead])
+    block = jnp.concatenate(
+        [parts_re.astype(f32) * scales[:, 0:1], parts_im.astype(f32) * scales[:, 1:2]], axis=2
+    ).reshape(length, 2 * lead)
+    big, small = coarse[:, :, None, dirs:], fine[:, None, :, dirs:]
+    steer = jnp.concatenate(
+        [big[0] * small[0] - big[1] * small[1], big[1] * small[0] + big[0] * small[1]], axis=2
+    ).reshape(length, 2 * dirs)
+    wide = lax.dot_general(
+        block, steer, (((0,), (0,)), ((), ())), precision=lax.Precision.HIGH, preferred_element_type=f32
     )
-    fine = jnp.stack(cis(jnp.arange(FINE, dtype=jnp.int32)[:, None] * odd[None, :], 2 * length))
-    q, cap, cross, parts, scale = product(inverse, snaps_all, snaps, applied, coarse, fine, 2 * snap)
-    cap, cross = lax.psum((cap, cross), "row")
-    parts_all = lax.all_gather(parts, "row", axis=0, tiled=True)
-    scales_all = lax.all_gather(scale, "row", axis=0, tiled=True)
+    cross = jnp.stack([
+        wide[:lead, :dirs] + wide[lead:, dirs:],
+        wide[:lead, dirs:] - wide[lead:, :dirs],
+    ])
+    cross = jnp.concatenate([cross, power], axis=1)
 
     fold, weights, spectrum = finish(cap, cross, q, applied, steps, window, length)
-    new_inverse = low_rank_update(inverse, fold, parts_all, scales_all)
+    new_inverse = low_rank_update(inverse, fold, parts_all)
     return new_inverse, weights, spectrum
 
 

time: 319 us -> 293 us (0.918)
  waiting for transfers between devices: 160 us -> 0 us
  Pallas kernels: 114 us -> 239 us
  other arithmetic: 6.21 us -> 29.1 us
  blocking collectives: 20.9 us -> 0 us
  matrix products: 1.17 us -> 19.9 us
  between operations: 13.9 us -> 0.8 us
    pallas_call x1 -> x4, Pallas kernels: 21.2 us -> 146 us  [the longest x2 102 us: gather(): pl.pallas_call(functools.partial(gather_kernel, chips), in_specs=[pl.Bloc...]
    psum x1 -> x0, waiting for transfers between devices: 81.1 us -> none  [on_device(): cap, cross = lax.psum((cap, cross), 'row')]
    all_gather x2 -> x0, waiting for transfers between devices: 78.3 us -> none  [the longest x1 50.2 us: on_device(): snaps_all = lax.all_gather(snaps, 'row', axis=1, tiled=True)]
    all_gather x1 -> x0, blocking collectives: 20.9 us -> none  [on_device(): scales_all = lax.all_gather(scale, 'row', axis=0, tiled=True)]
    dot_general x0 -> x1, matrix products: none -> 18.8 us  [on_device(): lax.dot_general(block, steer, (((0,), (0,)), ((), ())), precision=lax.Pre...]
    sub x0 -> x1, other arithmetic: none -> 7.15 us  [on_device(): big[0] * small[0] - big[1] * small[1]]
    concatenate x0 -> x3, other arithmetic: none -> 6.63 us  [the longest x1 4.56 us: on_device(): jnp.concatenate([parts_re.astype(f32) * scales[:, 0:1], parts_im.astype(f...]
    sin x0 -> x1, other arithmetic: none -> 4.15 us  [cis(): return (jnp.cos(phase), jnp.sin(phase))]
  transfers between devices with their start and end apart: 3 -> 0, of which waited for: 3 -> 0; matrix products, arithmetic and copies ran while one was open for 2% -> 0% of each run, Pallas kernels for 22% -> 0%
where the time goes in v2:
time: 293 us; the launch traced here: 292 us
  Pallas kernels  239 us (82%)
  other arithmetic  29.1 us (10%)
  matrix products  19.9 us (7%)
  local copies, waits for them, and re-layouts  3.17 us (1%)
    pallas_call x2, Pallas kernels, gather(): pl.pallas_call(functools.partial(gather_kernel, chips), in_specs=[pl.Bloc...  102 us
    pallas_call x1, Pallas kernels, finish(): pl.pallas_call(functools.partial(finish_kernel, steps, window, length), i...  48.3 us
    pallas_call x1, Pallas kernels, sums(): pl.pallas_call(functools.partial(sums_kernel, blocks), grid=(blocks,), in...  26.1 us
    pallas_call x1, Pallas kernels, low_rank_update(): pl.pallas_call(update_kernel, grid=(length // rows,), in_specs=[pl.BlockS...  23.3 us
    pallas_call x1, Pallas kernels, steer_product(): pl.pallas_call(functools.partial(steer_kernel, blocks), grid=(blocks,), i...  21.2 us
    dot_general x1, matrix products, on_device(): lax.dot_general(block, steer, (((0,), (0,)), ((), ())), precision=lax.Pre...  18.8 us
    pallas_call x1, Pallas kernels, product(): pl.pallas_call(functools.partial(product_kernel, blocks), grid=(blocks,),...  17.9 us
    sub x1, other arithmetic, on_device(): big[0] * small[0] - big[1] * small[1]  7.15 us

profile of v2, /device:TPU:0, one launch (start us, length us, event | category | flops | bytes accessed | tf_op | source)
XLA Modules:
  0.0 292.1 jit_solution(13053519019611524385)
XLA Ops:
  0.7 1.2 copy-done
  1.9 0.7 multiply_bitcast_fusion
  2.9 0.6 pad_maximum_fusion.6.turn_ref
  4.0 0.7 pad_maximum_fusion.4
  4.7 1.2 fusion.4
  6.2 1.0 pad_maximum_fusion.3
  7.8 0.9 copy.12
  8.6 2.1 fusion.19
  10.7 1.1 pad_maximum_fusion.2.coarse_ref
  11.8 21.2 %shard_map.77.applied_ref = f32[2,256,1024]{2,1,0:T(8,128)} custom-call(f32[2,256,4096]{2,1,0:T(8,128)} %inv_ref.3, f32[2,256,4096]{2,1,0:T(8,128)} %inv_ref.3, f32[2,128,1024]{2,1,0:T(8,128)} %pad_maximum_fusion.2.coarse_ref, f32[2,16,1024]{2,1,0:T(8,128)} %get-tuple-element.39.fine_ref, f32[2,1024]{1,0:T(2,128)} %pad_maximum_fusion.6.turn_ref), custom_call_target="tpu_custom_call" | custom-call | flops 12884901888 | bytes 8388608 | tf_op jit(solution)/shard_map/pallas_call | solution.py:189
  33.1 4.1 %fusion.15 = (f32[1,256,1024]{2,1,0:T(8,128)S(1)}, f32[1,256,1024]{2,1,0:T(8,128)S(1)}) fusion(s32[1024]{0:T(1024)S(1)} %bitcast.49, s32[256]{0:T(256)S(1)} %iota_multiply_fusion), kind=kLoop, calls=%fused_computation.41 | loop fusion | flops 3670016 | bytes 2102272 | tf_op jit(solution)/shard_map/sin | solution.py:37
  37.2 0.7 fusion.20.coarse_ref
  38.0 51.8 %shard_map.76.all_ref.snaps_ref = bf16[16,512,512]{2,1,0:T(8,128)(2,1)} custom-call(bf16[512,512]{1,0:T(8,128)(2,1)} %bitcast.44), custom_call_target="tpu_custom_call" | custom-call | bytes 16777216 | tf_op jit(solution)/shard_map/pallas_call | solution.py:112
  89.8 17.9 %shard_map.78 = (f32[2,256,512]{2,1,0:T(8,128)}, s32[272,512]{1,0:T(8,128)}) custom-call(f32[2,256,4096]{2,1,0:T(8,128)} %inv_ref.3, bf16[16,512,512]{2,1,0:T(8,128)(2,1)} %shard_map.76.all_ref.snaps_ref, f32[2,256,1024]{2,1,0:T(8,128)} %shard_map.77.applied_ref, f32[2,16,1024]{2,1,0:T(8,128)} %fusion.20.coarse_ref, f32[2,16,1024]{2,1,0:T(8,128)} %get-tuple-element.40.fine_ref), custom_call_target="tpu_custom_call" | custom-call | flops 8589934592 | bytes 16777216 | tf_op jit(solution)/shard_map/pallas_call | solution.py:440
  107.7 50.5 %shard_map.79.parts_ref.part_ref = s32[16,272,512]{2,1,0:T(8,128)} custom-call(s32[272,512]{1,0:T(8,128)} %get-tuple-element.10.x_ref), custom_call_target="tpu_custom_call" | custom-call | bytes 17825792 | tf_op jit(solution)/shard_map/pallas_call | solution.py:112
  158.2 26.1 %shard_map.80 = (f32[2,512,512]{2,1,0:T(8,128)}, f32[2,8,512]{2,1,0:T(8,128)}) custom-call(s32[16,272,512]{2,1,0:T(8,128)} %shard_map.79.parts_ref.part_ref, bf16[16,512,512]{2,1,0:T(8,128)(2,1)} %shard_map.76.all_ref.snaps_ref), custom_call_target="tpu_custom_call" | custom-call | tf_op jit(solution)/shard_map/pallas_call | solution.py:496
  184.2 0.9 multiply_exponential_fusion
  185.2 3.5 %convert_multiply_fusion.1 = (f32[16,256,256]{2,1,0:T(8,128)S(1)}, f32[16,256,256]{2,1,0:T(8,128)S(1)}) fusion(s32[16,272,512]{2,1,0:T(8,128)} %shard_map.79.parts_ref.part_ref, f32[16,256]{1,0:T(8,128)S(1)} %bitcast.50, f32[16,256]{1,0:T(8,128)S(1)} %bitcast.51), kind=kLoop, calls=%fused_computation.8 | loop fusion | flops 8388608 | bytes 12615680 | tf_op jit(solution)/shard_map/mul | solution.py:541
  188.7 4.6 %pad_maximum_fusion = f32[16,256,512]{2,1,0:T(8,128)} fusion(f32[16,256,256]{2,1,0:T(8,128)S(1)} %get-tuple-element.20, f32[16,256,256]{2,1,0:T(8,128)S(1)} %get-tuple-element.19), kind=kLoop, calls=%fused_computation.4 | loop fusion | flops 2097152 | bytes 16777216 | tf_op jit(solution)/shard_map/concatenate | solution.py:540
  193.2 7.1 %multiply_subtract_fusion = (f32[256,16,512]{2,1,0:T(8,128)}, f32[256,16,512]{2,1,0:T(8,128)}) fusion(f32[16,512]{1,0:T(8,128)S(1)} %get-tuple-element.41, f32[256,512]{1,0:T(8,128)S(1)} %get-tuple-element.43, f32[16,512]{1,0:T(8,128)S(1)} %get-tuple-element.42, f32[256,512]{1,0:T(8,128)S(1)} %get-tuple-element.44), kind=kLoop, calls=%fused_computation.6 | loop fusion | flops 12582912 | bytes 17891328 | tf_op jit(solution)/shard_map/sub | solution.py:545
  200.4 18.8 %fusion = f32[512,1024]{1,0:T(8,128)S(1)} fusion(f32[4096,512]{1,0:T(8,128)} %bitcast.41, f32[4096,512]{1,0:T(8,128)} %bitcast.43, f32[4096,512]{1,0:T(8,128)} %bitcast.42), kind=kOutput, calls=%fused_computation | convolution fusion | flops 12889096192 | bytes 27262976 | tf_op jit(solution)/shard_map/dot_general | solution.py:547
  219.4 1.1 pad_maximum_fusion.1.cross_ref
  220.4 48.3 %shard_map.81 = (f32[2,256,512]{2,1,0:T(8,128)}, f32[2,2,256,512]{3,2,1,0:T(8,128)}, f32[2,512]{1,0:T(2,128)}) custom-call(f32[2,512,512]{2,1,0:T(8,128)} %get-tuple-element.11.cap_ref, f32[2,264,512]{2,1,0:T(8,128)} %pad_maximum_fusion.1.cross_ref, f32[2,256,512]{2,1,0:T(8,128)} %get-tuple-element.13.q_ref, f32[2,256,1024]{2,1,0:T(8,128)} %shard_map.77.applied_ref), custom_call_target="tpu_custom_call" | custom-call | flops 49999998976 | bytes 10000000 | tf_op jit(solution)/shard_map/pallas_call | solution.py:335
  268.8 23.3 %shard_map.82 = f32[2,256,4096]{2,1,0:T(8,128)} custom-call(f32[2,256,4096]{2,1,0:T(8,128)} %inv_ref.3, f32[2,256,512]{2,1,0:T(8,128)} %get-tuple-element.14.fold_ref, s32[16,272,512]{2,1,0:T(8,128)} %shard_map.79.parts_ref.part_ref), custom_call_target="tpu_custom_call" | custom-call | flops 12884901888 | bytes 16777216 | tf_op jit(solution)/shard_map/pallas_call | solution.py:366
  (22 shorter events, 2.0 us)
Async XLA Ops:
  0.6 1.2 copy-start
  200.4 19.0 %copy-start.2 = (f32[2,8,512]{2,1,0:T(8,128)S(1)}, f32[2,8,512]{2,1,0:T(8,128)}, u32[]{:S(2)}) copy-start(f32[2,8,512]{2,1,0:T(8,128)} %get-tuple-element.12) | copy-start | bytes 98308
  268.8 23.3 %copy-start.1 = (bf16[2,256,1024]{2,1,0:T(8,128)(2,1)S(1)}, bf16[2,256,1024]{2,1,0:T(8,128)(2,1)}, u32[]{:S(2)}) copy-start(bf16[2,256,1024]{2,1,0:T(8,128)(2,1)} %param.6) | copy-start | bytes 3145732
